TPU v7x, 32 devices: a whole 2x2x4 slice. The times are simulated.
32 devices in a mesh: row: 16 (over z, y, x), rep: 2 (over core).
Axes of the slice: x: 2, y: 2, z: 4, core: 2. Of those that a mesh axis runs over, the one named last changes fastest.
Arguments:
- features: bfloat16 [8192, 256], P('row'), may hold values from -6 to 6
- weight: bfloat16 [256, 256], replicated, may hold values from -0.375 to 0.375
- bias: float32 [256], replicated, may hold values from -3 to 3
- cotangent: bfloat16 [8192, 256], P(('row', 'rep')), may hold values from -14 to 14
- tile_values: bfloat16 [16, 16, 8, 128, 128], P('row', 'rep'), may hold values from -0.125 to 0.125
- tile_index: int32 [16, 16, 8, 2], P('row', 'rep'), may hold values from 0 to 3
- tile_count: int32 [16, 16], P('row', 'rep'), may hold values from 0 to 8, as said below
- rev_values: bfloat16 [16, 16, 8, 128, 128], P('row', 'rep'), may hold values from -0.125 to 0.125
- rev_index: int32 [16, 16, 8, 2], P('row', 'rep'), may hold values from 0 to 3
- rev_count: int32 [16, 16], P('row', 'rep'), may hold values from 0 to 8, as said below
Outputs:
- activations: bfloat16 [8192, 256], P(('row', 'rep'))
- grad_features: bfloat16 [8192, 256], P(('row', 'rep'))
- grad_weight: float32 [256, 256], replicated
- grad_bias: float32 [256], replicated
Inputs may be any that keep to these rules, and one draw needn't show every extreme that they name: Slots t < tile_count[a, d] are used; some slab pair uses all 8 slots in every draw. Slots t < rev_count[a, d] are used; some slab pair uses all 8 slots in every draw.
All inputs are finite; a program needn't handle non-finite values.
Results may differ from a plain program's by a relative error of at most 0.006.
Values may be sent and summed in bfloat16 or wider, within the bound.
A program may use at most 64 MiB of HBM per device.

v0:
```python
import jax
import jax.numpy as jnp
from jax import lax
from jax.sharding import PartitionSpec as P

TILE = 128
BLOCKS = 4


def passed_along(value, axis, steps):
    count = lax.axis_size(axis)
    pairs = [(source, (source + steps) % count) for source in range(count)]
    return lax.ppermute(value, axis, pairs)


def section_term(current, tile_block, slot_index, counts):
    blocks = current.reshape(BLOCKS, TILE, current.shape[1])
    sources = jnp.take(blocks, slot_index[:, 1], axis=0)
    product = jnp.einsum("tab,tbf->taf", tile_block, sources, preferred_element_type=jnp.float32)
    usable = jnp.arange(slot_index.shape[0], dtype=jnp.int32) < counts
    placing = (
        (slot_index[:, 0][None, :] == jnp.arange(BLOCKS, dtype=jnp.int32)[:, None])
        & usable[None, :]
    ).astype(jnp.float32)
    return jnp.einsum("nt,taf->naf", placing, product, precision=lax.Precision.HIGHEST)


def first_source(source, sections):
    rep_index = lax.axis_index("rep")
    groups = lax.axis_size("rep")
    current = source
    for shift_bit in range(groups.bit_length() - 1):
        shifted = passed_along(current, "row", -(sections << shift_bit))
        current = jnp.where(rep_index >> shift_bit & 1 == 1, shifted, current)
    return current


def apply_tiles(source, values, slot_index, counts):
    sections = values.shape[1]
    current = first_source(source, sections)
    summed_rows = jnp.zeros((BLOCKS, TILE, source.shape[1]), jnp.float32)
    for section in range(sections):
        if section > 0:
            current = passed_along(current, "row", -1)
        summed_rows = summed_rows + section_term(
            current, values[0, section], slot_index[0, section], counts[0, section]
        )
    return summed_rows.reshape(source.shape[0], source.shape[1])


def reduce_part(partial_rows):
    return lax.psum(partial_rows, "rep")


def own_rows(matrix):
    share_size = matrix.shape[0] // lax.axis_size("rep")
    return lax.dynamic_slice_in_dim(matrix, lax.axis_index("rep") * share_size, share_size, 0)


def activate(preact, cotangent):
    sigmoid_pre = jax.nn.sigmoid(preact)
    activations = (preact * sigmoid_pre).astype(jnp.bfloat16)
    grad_pre = (
        cotangent.astype(jnp.float32) * sigmoid_pre * (1.0 + preact * (1.0 - sigmoid_pre))
    ).astype(jnp.bfloat16)
    return (activations, grad_pre)


def local(
    features,
    weight,
    bias,
    cotangent,
    tile_values,
    tile_index,
    tile_count,
    rev_values,
    rev_index,
    rev_count,
):
    node_total = features.shape[0] * lax.axis_size("row")
    grad_scale = float(node_total) ** (-0.5)
    summed = reduce_part(apply_tiles(features, tile_values, tile_index, tile_count))
    mixed_all = summed.astype(jnp.bfloat16)
    preact_all = jnp.dot(mixed_all, weight, preferred_element_type=jnp.float32) + bias
    cotangent_all = lax.all_gather(cotangent, "rep", axis=0, tiled=True)
    activ_all, grad_all = activate(preact_all, cotangent_all)
    image = jnp.einsum("ng,fg->nf", grad_all, weight, preferred_element_type=jnp.float32).astype(
        jnp.bfloat16
    )
    mixed_rows = own_rows(mixed_all)
    grad_pre = own_rows(grad_all)
    activations = own_rows(activ_all)
    weight_term = jnp.einsum("nf,ng->fg", mixed_rows, grad_pre, preferred_element_type=jnp.float32)
    bias_term = jnp.sum(grad_pre.astype(jnp.float32), axis=0)
    grad_weight, grad_bias = lax.psum((weight_term, bias_term), ("row", "rep"))
    back_rows = reduce_part(apply_tiles(image, rev_values, rev_index, rev_count))
    back_rows = own_rows(back_rows)
    return (
        activations,
        back_rows.astype(jnp.bfloat16),
        grad_weight * grad_scale,
        grad_bias * grad_scale,
    )


def solution(mesh):
    placed = (
        P("row", None),
        P(),
        P(),
        P(("row", "rep"), None),
        P("row", "rep", None, None, None),
        P("row", "rep", None, None),
        P("row", "rep"),
        P("row", "rep", None, None, None),
        P("row", "rep", None, None),
        P("row", "rep"),
    )
    return jax.shard_map(
        local,
        mesh=mesh,
        in_specs=placed,
        out_specs=(P(("row", "rep"), None), P(("row", "rep"), None), P(), P()),
        check_vma=False,
    )
```

profile of v0, /device:TPU:0, one launch (start us, length us, event | category | flops | bytes accessed | tf_op | source)
XLA Modules:
  0.0 381.1 jit_solution(8210804947538525664)
XLA Ops:
  7.2 4.1 %collective-permute-start = (bf16[512,256]{1,0:T(8,128)(2,1)}, bf16[512,256]{1,0:T(8,128)(2,1)S(1)}, u32[]{:S(2)}, u32[]{:S(2)}) collective-permute-start(bf16[512,256]{1,0:T(8,128)(2,1)} %param.12), channel_id=1, source_target_pairs={{0,16},{2,18},{4,20},{6,22},{8,24},{10,26},{12,28},{14,30},{16,0},... | collective-permute-start | bytes 786440 | tf_op jit(solution)/shard_map/ppermute | solution.py:13
  23.6 1.6 fusion.216
  25.8 1.2 iota_compare_fusion.30
  38.3 1.6 fusion.215
  49.1 1.3 iota_compare_fusion.17
  52.1 3.5 all_gather.3
  57.3 3.3 collective-permute-start.1
  61.1 1.4 fusion.48
  63.6 2.1 collective-permute-done.1
  66.3 1.4 fusion.46
  68.1 6.1 %collective-permute-start.2 = (bf16[512,256]{1,0:T(8,128)(2,1)S(1)}, bf16[512,256]{1,0:T(8,128)(2,1)S(1)}, u32[]{:S(2)}, u32[]{:S(2)}) collective-permute-start(bf16[512,256]{1,0:T(8,128)(2,1)S(1)} %collective-permute-done.1), channel_id=1, source_target_pairs={{0,30},{2,0},{4,2},{6,4},{8,6},{10,8},{12,10},{14,12},{16,14},{18,... | collective-permute-start | bytes 786440 | tf_op jit(solution)/shard_map/ppermute | solution.py:13
  74.3 1.3 convolution_add_fusion.13
  75.6 2.9 collective-permute-done.2
  79.2 1.4 fusion.44
  81.1 6.1 %collective-permute-start.3 = (bf16[512,256]{1,0:T(8,128)(2,1)S(1)}, bf16[512,256]{1,0:T(8,128)(2,1)S(1)}, u32[]{:S(2)}, u32[]{:S(2)}) collective-permute-start(bf16[512,256]{1,0:T(8,128)(2,1)S(1)} %copy-done.2), channel_id=1, source_target_pairs={{0,30},{2,0},{4,2},{6,4},{8,6},{10,8},{12,10},{14,12},{16,14},{18,... | collective-permute-start | bytes 786440 | tf_op jit(solution)/shard_map/ppermute | solution.py:13
  87.3 1.3 convolution_add_fusion.12
  88.5 2.6 collective-permute-done.3
  91.9 1.4 fusion.42
  93.8 6.1 %collective-permute-start.4 = (bf16[512,256]{1,0:T(8,128)(2,1)S(1)}, bf16[512,256]{1,0:T(8,128)(2,1)S(1)}, u32[]{:S(2)}, u32[]{:S(2)}) collective-permute-start(bf16[512,256]{1,0:T(8,128)(2,1)S(1)} %copy-done.4), channel_id=1, source_target_pairs={{0,30},{2,0},{4,2},{6,4},{8,6},{10,8},{12,10},{14,12},{16,14},{18,... | collective-permute-start | bytes 786440 | tf_op jit(solution)/shard_map/ppermute | solution.py:13
  99.9 1.3 convolution_add_fusion.11
  101.2 2.6 collective-permute-done.4
  104.6 1.4 fusion.40
  106.5 6.1 %collective-permute-start.5 = (bf16[512,256]{1,0:T(8,128)(2,1)S(1)}, bf16[512,256]{1,0:T(8,128)(2,1)S(1)}, u32[]{:S(2)}, u32[]{:S(2)}) collective-permute-start(bf16[512,256]{1,0:T(8,128)(2,1)S(1)} %copy-done.6), channel_id=1, source_target_pairs={{0,30},{2,0},{4,2},{6,4},{8,6},{10,8},{12,10},{14,12},{16,14},{18,... | collective-permute-start | bytes 786440 | tf_op jit(solution)/shard_map/ppermute | solution.py:13
  112.6 1.3 convolution_add_fusion.10
  113.9 2.6 collective-permute-done.5
  117.2 1.4 fusion.38
  119.1 6.1 %collective-permute-start.6 = (bf16[512,256]{1,0:T(8,128)(2,1)S(1)}, bf16[512,256]{1,0:T(8,128)(2,1)S(1)}, u32[]{:S(2)}, u32[]{:S(2)}) collective-permute-start(bf16[512,256]{1,0:T(8,128)(2,1)S(1)} %copy-done.8), channel_id=1, source_target_pairs={{0,30},{2,0},{4,2},{6,4},{8,6},{10,8},{12,10},{14,12},{16,14},{18,... | collective-permute-start | bytes 786440 | tf_op jit(solution)/shard_map/ppermute | solution.py:13
  125.3 1.3 convolution_add_fusion.9
  126.6 2.6 collective-permute-done.6
  129.9 1.4 fusion.36
  131.8 6.3 %collective-permute-start.7 = (bf16[512,256]{1,0:T(8,128)(2,1)S(1)}, bf16[512,256]{1,0:T(8,128)(2,1)S(1)}, u32[]{:S(2)}, u32[]{:S(2)}) collective-permute-start(bf16[512,256]{1,0:T(8,128)(2,1)S(1)} %copy-done.10), channel_id=1, source_target_pairs={{0,30},{2,0},{4,2},{6,4},{8,6},{10,8},{12,10},{14,12},{16,14},{18,... | collective-permute-start | bytes 786440 | tf_op jit(solution)/shard_map/ppermute | solution.py:13
  138.1 1.3 convolution_add_fusion.8
  139.4 2.6 collective-permute-done.7
  142.7 1.4 fusion.34
  145.4 4.8 %all-reduce.5 = bf16[512,256]{1,0:T(8,128)(2,1)S(1)} all-reduce(f32[512,256]{1,0:T(8,128)S(1)} %bitcast.296), channel_id=1, replica_groups=mesh['row'=16,'rep'=2] {'rep'}, use_global_device_ids=true, to_apply=%region_0.2 | all-reduce | flops 131072 | bytes 786432 | tf_op jit(solution)/shard_map/psum | solution.py:52
  152.0 43.5 %psum.31 = f32[256]{0:T(256)S(1)} all-reduce(f32[256]{0:T(256)S(1)} %convert_reduce_fusion), channel_id=1, replica_groups=mesh['row'=16,'rep'=2] {'row','rep'}, use_global_device_ids=true, to_apply=%region_4.6 | all-reduce | flops 256 | bytes 2048 | tf_op jit(solution)/shard_map/psum | solution.py:96
  196.7 82.9 %all-reduce.4.cloned.1.call-done = f32[256,256]{1,0:T(8,128)} async-done(((f32[256,256]{1,0:T(8,128)}), f32[256,256]{1,0:T(8,128)}) %all-reduce.4.cloned.1.call-update) | async-done | bytes 262160 | tf_op jit(solution)/shard_map/psum | solution.py:96
  279.6 1.7 broadcast_multiply_fusion
  281.3 3.3 collective-permute-start.9
  285.4 1.4 fusion.32
  287.9 1.5 collective-permute-done.9
  290.1 1.4 fusion.30
  292.0 6.1 %collective-permute-start.10 = (bf16[512,256]{1,0:T(8,128)(2,1)S(1)}, bf16[512,256]{1,0:T(8,128)(2,1)S(1)}, u32[]{:S(2)}, u32[]{:S(2)}) collective-permute-start(bf16[512,256]{1,0:T(8,128)(2,1)S(1)} %collective-permute-done.9), channel_id=1, source_target_pairs={{0,30},{2,0},{4,2},{6,4},{8,6},{10,8},{12,10},{14,12},{16,14},{18,... | collective-permute-start | bytes 786440 | tf_op jit(solution)/shard_map/ppermute | solution.py:13
  298.1 1.3 convolution_add_fusion.6
  299.4 2.6 collective-permute-done.10
  302.7 1.4 fusion.28
  304.7 6.1 %collective-permute-start.11 = (bf16[512,256]{1,0:T(8,128)(2,1)S(1)}, bf16[512,256]{1,0:T(8,128)(2,1)S(1)}, u32[]{:S(2)}, u32[]{:S(2)}) collective-permute-start(bf16[512,256]{1,0:T(8,128)(2,1)S(1)} %copy-done.12), channel_id=1, source_target_pairs={{0,30},{2,0},{4,2},{6,4},{8,6},{10,8},{12,10},{14,12},{16,14},{18,... | collective-permute-start | bytes 786440 | tf_op jit(solution)/shard_map/ppermute | solution.py:13
  310.8 1.3 convolution_add_fusion.5
  312.1 2.6 collective-permute-done.11
  315.4 1.4 fusion.26
  317.3 6.1 %collective-permute-start.12 = (bf16[512,256]{1,0:T(8,128)(2,1)S(1)}, bf16[512,256]{1,0:T(8,128)(2,1)S(1)}, u32[]{:S(2)}, u32[]{:S(2)}) collective-permute-start(bf16[512,256]{1,0:T(8,128)(2,1)S(1)} %copy-done.14), channel_id=1, source_target_pairs={{0,30},{2,0},{4,2},{6,4},{8,6},{10,8},{12,10},{14,12},{16,14},{18,... | collective-permute-start | bytes 786440 | tf_op jit(solution)/shard_map/ppermute | solution.py:13
  323.5 1.3 convolution_add_fusion.4
  324.7 2.6 collective-permute-done.12
  328.1 1.4 fusion.24
  330.0 6.4 %collective-permute-start.13 = (bf16[512,256]{1,0:T(8,128)(2,1)S(1)}, bf16[512,256]{1,0:T(8,128)(2,1)S(1)}, u32[]{:S(2)}, u32[]{:S(2)}) collective-permute-start(bf16[512,256]{1,0:T(8,128)(2,1)S(1)} %copy-done.16), channel_id=1, source_target_pairs={{0,30},{2,0},{4,2},{6,4},{8,6},{10,8},{12,10},{14,12},{16,14},{18,... | collective-permute-start | bytes 786440 | tf_op jit(solution)/shard_map/ppermute | solution.py:13
  337.5 2.7 collective-permute-done.13
  340.9 1.4 fusion.22
  342.8 6.1 %collective-permute-start.14 = (bf16[512,256]{1,0:T(8,128)(2,1)S(1)}, bf16[512,256]{1,0:T(8,128)(2,1)S(1)}, u32[]{:S(2)}, u32[]{:S(2)}) collective-permute-start(bf16[512,256]{1,0:T(8,128)(2,1)S(1)} %copy-done.18), channel_id=1, source_target_pairs={{0,30},{2,0},{4,2},{6,4},{8,6},{10,8},{12,10},{14,12},{16,14},{18,... | collective-permute-start | bytes 786440 | tf_op jit(solution)/shard_map/ppermute | solution.py:13
  349.6 3.3 collective-permute-done.14
  353.6 1.4 fusion.20
  355.5 6.1 %collective-permute-start.15 = (bf16[512,256]{1,0:T(8,128)(2,1)S(1)}, bf16[512,256]{1,0:T(8,128)(2,1)S(1)}, u32[]{:S(2)}, u32[]{:S(2)}) collective-permute-start(bf16[512,256]{1,0:T(8,128)(2,1)S(1)} %copy-done.20), channel_id=1, source_target_pairs={{0,30},{2,0},{4,2},{6,4},{8,6},{10,8},{12,10},{14,12},{16,14},{18,... | collective-permute-start | bytes 786440 | tf_op jit(solution)/shard_map/ppermute | solution.py:13
  362.3 3.3 collective-permute-done.15
  366.1 1.4 fusion.18
  368.7 4.8 %all-reduce.6 = bf16[512,256]{1,0:T(8,128)(2,1)S(1)} all-reduce(f32[512,256]{1,0:T(8,128)S(1)} %bitcast.297), channel_id=1, replica_groups=mesh['row'=16,'rep'=2] {'rep'}, use_global_device_ids=true, to_apply=%region_1.3 | all-reduce | flops 131072 | bytes 786432 | tf_op jit(solution)/shard_map/psum | solution.py:52
  (185 shorter events, 63.9 us)
Async XLA Ops:
  7.2 143.1 %copy-start = (bf16[256,256]{1,0:T(8,128)(2,1)S(1)}, bf16[256,256]{1,0:T(8,128)(2,1)}, u32[]{:S(2)}) copy-start(bf16[256,256]{1,0:T(8,128)(2,1)} %param.13) | copy-start | bytes 393220
  7.2 272.4 %all-reduce.4.cloned.1.call-start = ((), (), s32[]{:S(2)}) async-start(), calls=%async_computation | async-start | bytes 524288 | tf_op jit(solution)/shard_map/psum | solution.py:96
  7.2 49.0 %collective-permute-start = (bf16[512,256]{1,0:T(8,128)(2,1)}, bf16[512,256]{1,0:T(8,128)(2,1)S(1)}, u32[]{:S(2)}, u32[]{:S(2)}) collective-permute-start(bf16[512,256]{1,0:T(8,128)(2,1)} %param.12), channel_id=1, source_target_pairs={{0,16},{2,18},{4,20},{6,22},{8,24},{10,26},{12,28},{14,30},{16,0},... | collective-permute-start | bytes 786440 | tf_op jit(solution)/shard_map/ppermute | solution.py:13
  57.3 8.4 %collective-permute-start.1 = (bf16[512,256]{1,0:T(8,128)(2,1)S(1)}, bf16[512,256]{1,0:T(8,128)(2,1)S(1)}, u32[]{:S(2)}, u32[]{:S(2)}) collective-permute-start(bf16[512,256]{1,0:T(8,128)(2,1)S(1)} %broadcast_select_fusion.1), channel_id=1, source_target_pairs={{0,30},{2,0},{4,2},{6,4},{8,6},{10,8},{12,10},{14,12},{16,14},{18,... | collective-permute-start | bytes 786440 | tf_op jit(solution)/shard_map/ppermute | solution.py:13
  68.1 10.4 %collective-permute-start.2 = (bf16[512,256]{1,0:T(8,128)(2,1)S(1)}, bf16[512,256]{1,0:T(8,128)(2,1)S(1)}, u32[]{:S(2)}, u32[]{:S(2)}) collective-permute-start(bf16[512,256]{1,0:T(8,128)(2,1)S(1)} %collective-permute-done.1), channel_id=1, source_target_pairs={{0,30},{2,0},{4,2},{6,4},{8,6},{10,8},{12,10},{14,12},{16,14},{18,... | collective-permute-start | bytes 786440 | tf_op jit(solution)/shard_map/ppermute | solution.py:13
  78.5 0.7 copy-start.1
  79.2 1.9 copy-start.2
  81.1 10.0 %collective-permute-start.3 = (bf16[512,256]{1,0:T(8,128)(2,1)S(1)}, bf16[512,256]{1,0:T(8,128)(2,1)S(1)}, u32[]{:S(2)}, u32[]{:S(2)}) collective-permute-start(bf16[512,256]{1,0:T(8,128)(2,1)S(1)} %copy-done.2), channel_id=1, source_target_pairs={{0,30},{2,0},{4,2},{6,4},{8,6},{10,8},{12,10},{14,12},{16,14},{18,... | collective-permute-start | bytes 786440 | tf_op jit(solution)/shard_map/ppermute | solution.py:13
  91.2 0.7 copy-start.3
  91.9 1.9 copy-start.4
  93.8 10.0 %collective-permute-start.4 = (bf16[512,256]{1,0:T(8,128)(2,1)S(1)}, bf16[512,256]{1,0:T(8,128)(2,1)S(1)}, u32[]{:S(2)}, u32[]{:S(2)}) collective-permute-start(bf16[512,256]{1,0:T(8,128)(2,1)S(1)} %copy-done.4), channel_id=1, source_target_pairs={{0,30},{2,0},{4,2},{6,4},{8,6},{10,8},{12,10},{14,12},{16,14},{18,... | collective-permute-start | bytes 786440 | tf_op jit(solution)/shard_map/ppermute | solution.py:13
  103.8 0.7 copy-start.5
  104.5 1.9 copy-start.6
  106.5 10.0 %collective-permute-start.5 = (bf16[512,256]{1,0:T(8,128)(2,1)S(1)}, bf16[512,256]{1,0:T(8,128)(2,1)S(1)}, u32[]{:S(2)}, u32[]{:S(2)}) collective-permute-start(bf16[512,256]{1,0:T(8,128)(2,1)S(1)} %copy-done.6), channel_id=1, source_target_pairs={{0,30},{2,0},{4,2},{6,4},{8,6},{10,8},{12,10},{14,12},{16,14},{18,... | collective-permute-start | bytes 786440 | tf_op jit(solution)/shard_map/ppermute | solution.py:13
  116.5 0.7 copy-start.7
  117.2 1.9 copy-start.8
  119.1 10.0 %collective-permute-start.6 = (bf16[512,256]{1,0:T(8,128)(2,1)S(1)}, bf16[512,256]{1,0:T(8,128)(2,1)S(1)}, u32[]{:S(2)}, u32[]{:S(2)}) collective-permute-start(bf16[512,256]{1,0:T(8,128)(2,1)S(1)} %copy-done.8), channel_id=1, source_target_pairs={{0,30},{2,0},{4,2},{6,4},{8,6},{10,8},{12,10},{14,12},{16,14},{18,... | collective-permute-start | bytes 786440 | tf_op jit(solution)/shard_map/ppermute | solution.py:13
  129.2 0.7 copy-start.9
  129.9 1.9 copy-start.10
  131.8 10.2 %collective-permute-start.7 = (bf16[512,256]{1,0:T(8,128)(2,1)S(1)}, bf16[512,256]{1,0:T(8,128)(2,1)S(1)}, u32[]{:S(2)}, u32[]{:S(2)}) collective-permute-start(bf16[512,256]{1,0:T(8,128)(2,1)S(1)} %copy-done.10), channel_id=1, source_target_pairs={{0,30},{2,0},{4,2},{6,4},{8,6},{10,8},{12,10},{14,12},{16,14},{18,... | collective-permute-start | bytes 786440 | tf_op jit(solution)/shard_map/ppermute | solution.py:13
  142.7 1.9 copy-start.27
  142.7 1.9 copy-start.35
  144.6 5.6 %copy-start.21 = (bf16[512,256]{1,0:T(8,128)(2,1)S(1)}, bf16[512,256]{1,0:T(8,128)(2,1)}, u32[]{:S(2)}) copy-start(bf16[512,256]{1,0:T(8,128)(2,1)} %all_gather.3) | copy-start | bytes 786436
  144.6 5.6 %copy-start.36 = (f32[256]{0:T(256)S(1)}, f32[256]{0:T(256)}, u32[]{:S(2)}) copy-start(f32[256]{0:T(256)} %param.14) | copy-start | bytes 3076
  150.9 134.5 %copy-start.33 = (pred[8]{0:T(512)(128)(4,1)S(1)}, pred[8]{0:T(512)(128)(4,1)}, u32[]{:S(2)}) copy-start(pred[8]{0:T(512)(128)(4,1)} %get-tuple-element.19) | copy-start | bytes 28
  151.9 129.4 %collective-permute-start.8 = (bf16[512,256]{1,0:T(8,128)(2,1)S(1)}, bf16[512,256]{1,0:T(8,128)(2,1)S(1)}, u32[]{:S(2)}, u32[]{:S(2)}) collective-permute-start(bf16[512,256]{1,0:T(8,128)(2,1)S(1)} %convolution_convert_fusion), channel_id=1, source_target_pairs={{0,16},{2,18},{4,20},{6,22},{8,24},{10,26},{12,28},{14,30},{16,0},... | collective-permute-start | bytes 786440 | tf_op jit(solution)/shard_map/ppermute | solution.py:13
  281.3 8.1 %collective-permute-start.9 = (bf16[512,256]{1,0:T(8,128)(2,1)S(1)}, bf16[512,256]{1,0:T(8,128)(2,1)S(1)}, u32[]{:S(2)}, u32[]{:S(2)}) collective-permute-start(bf16[512,256]{1,0:T(8,128)(2,1)S(1)} %broadcast_select_fusion), channel_id=1, source_target_pairs={{0,30},{2,0},{4,2},{6,4},{8,6},{10,8},{12,10},{14,12},{16,14},{18,... | collective-permute-start | bytes 786440 | tf_op jit(solution)/shard_map/ppermute | solution.py:13
  285.3 1.9 copy-start.22
  285.3 1.9 copy-start.28
  286.7 3.4 copy-start.31
  292.0 10.0 %collective-permute-start.10 = (bf16[512,256]{1,0:T(8,128)(2,1)S(1)}, bf16[512,256]{1,0:T(8,128)(2,1)S(1)}, u32[]{:S(2)}, u32[]{:S(2)}) collective-permute-start(bf16[512,256]{1,0:T(8,128)(2,1)S(1)} %collective-permute-done.9), channel_id=1, source_target_pairs={{0,30},{2,0},{4,2},{6,4},{8,6},{10,8},{12,10},{14,12},{16,14},{18,... | collective-permute-start | bytes 786440 | tf_op jit(solution)/shard_map/ppermute | solution.py:13
  302.0 0.7 copy-start.11
  302.7 1.9 copy-start.12
  304.7 10.0 %collective-permute-start.11 = (bf16[512,256]{1,0:T(8,128)(2,1)S(1)}, bf16[512,256]{1,0:T(8,128)(2,1)S(1)}, u32[]{:S(2)}, u32[]{:S(2)}) collective-permute-start(bf16[512,256]{1,0:T(8,128)(2,1)S(1)} %copy-done.12), channel_id=1, source_target_pairs={{0,30},{2,0},{4,2},{6,4},{8,6},{10,8},{12,10},{14,12},{16,14},{18,... | collective-permute-start | bytes 786440 | tf_op jit(solution)/shard_map/ppermute | solution.py:13
  314.7 0.7 copy-start.13
  315.4 1.9 copy-start.14
  317.3 10.0 %collective-permute-start.12 = (bf16[512,256]{1,0:T(8,128)(2,1)S(1)}, bf16[512,256]{1,0:T(8,128)(2,1)S(1)}, u32[]{:S(2)}, u32[]{:S(2)}) collective-permute-start(bf16[512,256]{1,0:T(8,128)(2,1)S(1)} %copy-done.14), channel_id=1, source_target_pairs={{0,30},{2,0},{4,2},{6,4},{8,6},{10,8},{12,10},{14,12},{16,14},{18,... | collective-permute-start | bytes 786440 | tf_op jit(solution)/shard_map/ppermute | solution.py:13
  327.3 0.7 copy-start.15
  328.1 8.3 %copy-start.24 = (s32[8]{0:T(128)S(1)}, s32[8]{0:T(128)}, u32[]{:S(2)}) copy-start(s32[8]{0:T(128)} %get-tuple-element.83) | copy-start | bytes 100
  328.1 1.9 copy-start.16
  330.0 10.2 %collective-permute-start.13 = (bf16[512,256]{1,0:T(8,128)(2,1)S(1)}, bf16[512,256]{1,0:T(8,128)(2,1)S(1)}, u32[]{:S(2)}, u32[]{:S(2)}) collective-permute-start(bf16[512,256]{1,0:T(8,128)(2,1)S(1)} %copy-done.16), channel_id=1, source_target_pairs={{0,30},{2,0},{4,2},{6,4},{8,6},{10,8},{12,10},{14,12},{16,14},{18,... | collective-permute-start | bytes 786440 | tf_op jit(solution)/shard_map/ppermute | solution.py:13
  340.2 0.7 copy-start.17
  340.9 8.1 %copy-start.23 = (s32[8]{0:T(128)S(1)}, s32[8]{0:T(128)}, u32[]{:S(2)}) copy-start(s32[8]{0:T(128)} %get-tuple-element.82) | copy-start | bytes 100
  340.9 8.1 %copy-start.34 = (pred[8]{0:T(512)(128)(4,1)S(1)}, pred[8]{0:T(512)(128)(4,1)}, u32[]{:S(2)}) copy-start(pred[8]{0:T(512)(128)(4,1)} %iota_compare_fusion.18) | copy-start | bytes 28
  340.9 1.9 copy-start.18
  342.8 10.0 %collective-permute-start.14 = (bf16[512,256]{1,0:T(8,128)(2,1)S(1)}, bf16[512,256]{1,0:T(8,128)(2,1)S(1)}, u32[]{:S(2)}, u32[]{:S(2)}) collective-permute-start(bf16[512,256]{1,0:T(8,128)(2,1)S(1)} %copy-done.18), channel_id=1, source_target_pairs={{0,30},{2,0},{4,2},{6,4},{8,6},{10,8},{12,10},{14,12},{16,14},{18,... | collective-permute-start | bytes 786440 | tf_op jit(solution)/shard_map/ppermute | solution.py:13
  352.9 0.7 copy-start.19
  353.6 8.1 %copy-start.26 = (s32[8]{0:T(128)S(1)}, s32[8]{0:T(128)}, u32[]{:S(2)}) copy-start(s32[8]{0:T(128)} %get-tuple-element.81) | copy-start | bytes 100
  353.6 8.1 %copy-start.32 = (pred[8]{0:T(512)(128)(4,1)S(1)}, pred[8]{0:T(512)(128)(4,1)}, u32[]{:S(2)}) copy-start(pred[8]{0:T(512)(128)(4,1)} %iota_compare_fusion.17) | copy-start | bytes 28
  353.6 1.9 copy-start.20
  355.5 10.6 %copy-start.30 = (pred[8]{0:T(512)(128)(4,1)S(1)}, pred[8]{0:T(512)(128)(4,1)}, u32[]{:S(2)}) copy-start(pred[8]{0:T(512)(128)(4,1)} %get-tuple-element.5) | copy-start | bytes 28
  355.5 10.0 %collective-permute-start.15 = (bf16[512,256]{1,0:T(8,128)(2,1)S(1)}, bf16[512,256]{1,0:T(8,128)(2,1)S(1)}, u32[]{:S(2)}, u32[]{:S(2)}) collective-permute-start(bf16[512,256]{1,0:T(8,128)(2,1)S(1)} %copy-done.20), channel_id=1, source_target_pairs={{0,30},{2,0},{4,2},{6,4},{8,6},{10,8},{12,10},{14,12},{16,14},{18,... | collective-permute-start | bytes 786440 | tf_op jit(solution)/shard_map/ppermute | solution.py:13
  366.1 1.9 copy-start.25
  366.1 1.9 copy-start.29
Sparse Core Ops, SparseCore 0:
  152.1 127.4 all-reduce.3
where the time goes:
time: 382 us; the launch traced here: 381 us
  waiting for transfers between devices  119 us (31%)
  starting transfers between devices  84.8 us (22%)
  blocking collectives  56.7 us (15%)
  matrix products  40.4 us (11%)
  other arithmetic  35.9 us (9%)
  local copies, waits for them, and re-layouts  28.9 us (8%)
  between operations  15 us (4%)
    ppermute x16, starting transfers between devices, passed_along(): return lax.ppermute(value, axis, pairs)  84.7 us
    psum x1, waiting for transfers between devices, local(): grad_weight, grad_bias = lax.psum((weight_term, bias_term), ('row', 'rep'))  82.9 us
    psum x1, blocking collectives, local(): grad_weight, grad_bias = lax.psum((weight_term, bias_term), ('row', 'rep'))  43.5 us
    ppermute x16, waiting for transfers between devices, passed_along(): return lax.ppermute(value, axis, pairs)  36.6 us
    dot_general x16, matrix products, section_term(): jnp.einsum('tab,tbf->taf', tile_block, sources, preferred_element_type=jn...  22.4 us
    lt x16, other arithmetic, section_term(): usable = jnp.arange(slot_index.shape[0], dtype=jnp.int32) < counts  18.2 us
    dot_general x16, matrix products, section_term(): jnp.einsum('nt,taf->naf', placing, product, precision=lax.Precision.HIGHEST)  16.4 us
    gather x16, local copies, waits for them, and re-layouts, section_term(): sources = jnp.take(blocks, slot_index[:, 1], axis=0)  10.5 us
  transfers between devices with their start and end apart: 17, of which 15 were waited for; matrix products, arithmetic and copies ran while one was open for 17% of the time, Pallas kernels for 0%

commit v1 on v0

--- a/solution.py
+++ b/solution.py
@@ -93,7 +93,9 @@
     activations = own_rows(activ_all)
     weight_term = jnp.einsum("nf,ng->fg", mixed_rows, grad_pre, preferred_element_type=jnp.float32)
     bias_term = jnp.sum(grad_pre.astype(jnp.float32), axis=0)
-    grad_weight, grad_bias = lax.psum((weight_term, bias_term), ("row", "rep"))
+    grad_weight, grad_bias = lax.psum(
+        lax.psum((weight_term, bias_term), axis_name="rep"), axis_name="row"
+    )
     back_rows = reduce_part(apply_tiles(image, rev_values, rev_index, rev_count))
     back_rows = own_rows(back_rows)
     return (

time: 382 us -> 422 us (1.10)
  waiting for transfers between devices: 119 us -> 159 us
    psum x1 -> x2, waiting for transfers between devices: 82.9 us -> 118 us  [the longest x1 113 us: local(): lax.psum(lax.psum((weight_term, bias_term), axis_name='rep'), axis_name='...]
    ppermute x16, waiting for transfers between devices: 36.6 us -> 41.3 us  [passed_along(): return lax.ppermute(value, axis, pairs)]
  transfers between devices with their start and end apart: 17 -> 18, of which waited for: 15 -> 16; matrix products, arithmetic and copies ran while one was open for 17% -> 16% of each run, Pallas kernels for 0% -> 0%
where the time goes in v1:
time: 422 us; the launch traced here: 421 us
  waiting for transfers between devices  159 us (38%)
  starting transfers between devices  84.7 us (20%)
  blocking collectives  55.8 us (13%)
  matrix products  40.3 us (10%)
  other arithmetic  36.5 us (9%)
  local copies, waits for them, and re-layouts  28.9 us (7%)
  between operations  15 us (4%)
    psum x1, waiting for transfers between devices, local(): lax.psum(lax.psum((weight_term, bias_term), axis_name='rep'), axis_name='...  113 us
    ppermute x16, starting transfers between devices, passed_along(): return lax.ppermute(value, axis, pairs)  84.6 us
    psum x1, blocking collectives, local(): lax.psum(lax.psum((weight_term, bias_term), axis_name='rep'), axis_name='...  42.6 us
    ppermute x16, waiting for transfers between devices, passed_along(): return lax.ppermute(value, axis, pairs)  41.3 us
    dot_general x16, matrix products, section_term(): jnp.einsum('tab,tbf->taf', tile_block, sources, preferred_element_type=jn...  22.4 us
    lt x16, other arithmetic, section_term(): usable = jnp.arange(slot_index.shape[0], dtype=jnp.int32) < counts  18.3 us
    dot_general x16, matrix products, section_term(): jnp.einsum('nt,taf->naf', placing, product, precision=lax.Precision.HIGHEST)  16.3 us
    gather x16, local copies, waits for them, and re-layouts, section_term(): sources = jnp.take(blocks, slot_index[:, 1], axis=0)  10.5 us
  transfers between devices with their start and end apart: 18, of which 16 were waited for; matrix products, arithmetic and copies ran while one was open for 16% of the time, Pallas kernels for 0%

profile of v1, /device:TPU:0, one launch (start us, length us, event | category | flops | bytes accessed | tf_op | source)
XLA Modules:
  0.0 420.6 jit_solution(7674333644690898593)
XLA Ops:
  7.2 4.1 collective-permute-start
  23.5 1.6 fusion.216
  25.8 1.2 iota_compare_fusion.30
  29.5 1.3 iota_compare_fusion.28
  38.3 1.6 fusion.215
  51.0 3.5 all_gather.3
  56.1 3.3 collective-permute-start.1
  60.0 1.4 fusion.48
  62.5 2.1 collective-permute-done.1
  65.2 1.4 fusion.46
  67.0 6.1 %collective-permute-start.2 = (bf16[512,256]{1,0:T(8,128)(2,1)S(1)}, bf16[512,256]{1,0:T(8,128)(2,1)S(1)}, u32[]{:S(2)}, u32[]{:S(2)}) collective-permute-start(bf16[512,256]{1,0:T(8,128)(2,1)S(1)} %collective-permute-done.1), channel_id=1, source_target_pairs={{0,30},{2,0},{4,2},{6,4},{8,6},{10,8},{12,10},{14,12},{16,14},{18,... | collective-permute-start | bytes 786440 | tf_op jit(solution)/shard_map/ppermute | solution.py:13
  73.1 1.3 convolution_add_fusion.13
  74.4 2.9 collective-permute-done.2
  78.1 1.4 fusion.44
  80.0 6.1 %collective-permute-start.3 = (bf16[512,256]{1,0:T(8,128)(2,1)S(1)}, bf16[512,256]{1,0:T(8,128)(2,1)S(1)}, u32[]{:S(2)}, u32[]{:S(2)}) collective-permute-start(bf16[512,256]{1,0:T(8,128)(2,1)S(1)} %copy-done.2), channel_id=1, source_target_pairs={{0,30},{2,0},{4,2},{6,4},{8,6},{10,8},{12,10},{14,12},{16,14},{18,... | collective-permute-start | bytes 786440 | tf_op jit(solution)/shard_map/ppermute | solution.py:13
  86.1 1.3 convolution_add_fusion.12
  87.4 2.6 collective-permute-done.3
  90.8 1.4 fusion.42
  92.7 6.1 %collective-permute-start.4 = (bf16[512,256]{1,0:T(8,128)(2,1)S(1)}, bf16[512,256]{1,0:T(8,128)(2,1)S(1)}, u32[]{:S(2)}, u32[]{:S(2)}) collective-permute-start(bf16[512,256]{1,0:T(8,128)(2,1)S(1)} %copy-done.4), channel_id=1, source_target_pairs={{0,30},{2,0},{4,2},{6,4},{8,6},{10,8},{12,10},{14,12},{16,14},{18,... | collective-permute-start | bytes 786440 | tf_op jit(solution)/shard_map/ppermute | solution.py:13
  98.8 1.3 convolution_add_fusion.11
  100.1 2.6 collective-permute-done.4
  103.4 1.4 fusion.40
  105.4 6.1 %collective-permute-start.5 = (bf16[512,256]{1,0:T(8,128)(2,1)S(1)}, bf16[512,256]{1,0:T(8,128)(2,1)S(1)}, u32[]{:S(2)}, u32[]{:S(2)}) collective-permute-start(bf16[512,256]{1,0:T(8,128)(2,1)S(1)} %copy-done.6), channel_id=1, source_target_pairs={{0,30},{2,0},{4,2},{6,4},{8,6},{10,8},{12,10},{14,12},{16,14},{18,... | collective-permute-start | bytes 786440 | tf_op jit(solution)/shard_map/ppermute | solution.py:13
  111.5 1.3 convolution_add_fusion.10
  112.8 2.6 collective-permute-done.5
  116.1 1.4 fusion.38
  118.0 6.1 %collective-permute-start.6 = (bf16[512,256]{1,0:T(8,128)(2,1)S(1)}, bf16[512,256]{1,0:T(8,128)(2,1)S(1)}, u32[]{:S(2)}, u32[]{:S(2)}) collective-permute-start(bf16[512,256]{1,0:T(8,128)(2,1)S(1)} %copy-done.8), channel_id=1, source_target_pairs={{0,30},{2,0},{4,2},{6,4},{8,6},{10,8},{12,10},{14,12},{16,14},{18,... | collective-permute-start | bytes 786440 | tf_op jit(solution)/shard_map/ppermute | solution.py:13
  124.2 1.3 convolution_add_fusion.9
  125.4 2.6 collective-permute-done.6
  128.8 1.4 fusion.36
  130.7 6.3 %collective-permute-start.7 = (bf16[512,256]{1,0:T(8,128)(2,1)S(1)}, bf16[512,256]{1,0:T(8,128)(2,1)S(1)}, u32[]{:S(2)}, u32[]{:S(2)}) collective-permute-start(bf16[512,256]{1,0:T(8,128)(2,1)S(1)} %copy-done.10), channel_id=1, source_target_pairs={{0,30},{2,0},{4,2},{6,4},{8,6},{10,8},{12,10},{14,12},{16,14},{18,... | collective-permute-start | bytes 786440 | tf_op jit(solution)/shard_map/ppermute | solution.py:13
  137.0 1.3 convolution_add_fusion.8
  138.3 2.6 collective-permute-done.7
  141.6 1.4 fusion.34
  144.3 4.8 %all-reduce.9 = bf16[512,256]{1,0:T(8,128)(2,1)S(1)} all-reduce(f32[512,256]{1,0:T(8,128)S(1)} %bitcast.297), channel_id=1, replica_groups=mesh['row'=16,'rep'=2] {'rep'}, use_global_device_ids=true, to_apply=%region_0.2 | all-reduce | flops 131072 | bytes 786432 | tf_op jit(solution)/shard_map/psum | solution.py:52
  153.3 6.1 %collective-permute-done.8 = bf16[512,256]{1,0:T(8,128)(2,1)S(1)} collective-permute-done((bf16[512,256]{1,0:T(8,128)(2,1)S(1)}, bf16[512,256]{1,0:T(8,128)(2,1)S(1)}, u32[]{:S(2)}, u32[]{:S(2)}) %collective-permute-start.8) | collective-permute-done | bytes 262176 | tf_op jit(solution)/shard_map/ppermute | solution.py:13
  159.5 6.0 %collective-permute-start.9 = (bf16[512,256]{1,0:T(8,128)(2,1)S(1)}, bf16[512,256]{1,0:T(8,128)(2,1)S(1)}, u32[]{:S(2)}, u32[]{:S(2)}) collective-permute-start(bf16[512,256]{1,0:T(8,128)(2,1)S(1)} %broadcast_select_fusion), channel_id=1, source_target_pairs={{0,30},{2,0},{4,2},{6,4},{8,6},{10,8},{12,10},{14,12},{16,14},{18,... | collective-permute-start | bytes 786440 | tf_op jit(solution)/shard_map/ppermute | solution.py:13
  166.2 1.4 fusion.32
  168.1 4.7 %all-reduce.6.cloned.1.call-done = f32[256,256]{1,0:T(8,128)} async-done(((f32[256,256]{1,0:T(8,128)}), f32[256,256]{1,0:T(8,128)}) %all-reduce.6.cloned.1.call-update) | async-done | bytes 262160 | tf_op jit(solution)/shard_map/psum | solution.py:97
  173.4 113.3 %all-reduce.8.cloned.1.call-done = f32[256,256]{1,0:T(8,128)} async-done(((f32[256,256]{1,0:T(8,128)}), f32[256,256]{1,0:T(8,128)}) %all-reduce.8.cloned.1.call-update) | async-done | bytes 262160 | tf_op jit(solution)/shard_map/psum | solution.py:96
  286.8 1.7 broadcast_multiply_fusion
  289.2 1.4 fusion.30
  291.0 3.3 collective-permute-start.10
  294.3 1.3 convolution_add_fusion.6
  295.6 2.6 collective-permute-done.10
  298.9 1.4 fusion.28
  300.9 6.1 %collective-permute-start.11 = (bf16[512,256]{1,0:T(8,128)(2,1)S(1)}, bf16[512,256]{1,0:T(8,128)(2,1)S(1)}, u32[]{:S(2)}, u32[]{:S(2)}) collective-permute-start(bf16[512,256]{1,0:T(8,128)(2,1)S(1)} %copy-done.12), channel_id=1, source_target_pairs={{0,30},{2,0},{4,2},{6,4},{8,6},{10,8},{12,10},{14,12},{16,14},{18,... | collective-permute-start | bytes 786440 | tf_op jit(solution)/shard_map/ppermute | solution.py:13
  307.0 1.3 convolution_add_fusion.5
  308.3 2.6 collective-permute-done.11
  311.6 1.4 fusion.26
  313.5 6.1 %collective-permute-start.12 = (bf16[512,256]{1,0:T(8,128)(2,1)S(1)}, bf16[512,256]{1,0:T(8,128)(2,1)S(1)}, u32[]{:S(2)}, u32[]{:S(2)}) collective-permute-start(bf16[512,256]{1,0:T(8,128)(2,1)S(1)} %copy-done.14), channel_id=1, source_target_pairs={{0,30},{2,0},{4,2},{6,4},{8,6},{10,8},{12,10},{14,12},{16,14},{18,... | collective-permute-start | bytes 786440 | tf_op jit(solution)/shard_map/ppermute | solution.py:13
  320.9 2.7 collective-permute-done.12
  324.3 1.4 fusion.24
  326.2 6.4 %collective-permute-start.13 = (bf16[512,256]{1,0:T(8,128)(2,1)S(1)}, bf16[512,256]{1,0:T(8,128)(2,1)S(1)}, u32[]{:S(2)}, u32[]{:S(2)}) collective-permute-start(bf16[512,256]{1,0:T(8,128)(2,1)S(1)} %copy-done.16), channel_id=1, source_target_pairs={{0,30},{2,0},{4,2},{6,4},{8,6},{10,8},{12,10},{14,12},{16,14},{18,... | collective-permute-start | bytes 786440 | tf_op jit(solution)/shard_map/ppermute | solution.py:13
  333.8 2.7 collective-permute-done.13
  337.2 1.4 fusion.22
  339.1 6.1 %collective-permute-start.14 = (bf16[512,256]{1,0:T(8,128)(2,1)S(1)}, bf16[512,256]{1,0:T(8,128)(2,1)S(1)}, u32[]{:S(2)}, u32[]{:S(2)}) collective-permute-start(bf16[512,256]{1,0:T(8,128)(2,1)S(1)} %copy-done.18), channel_id=1, source_target_pairs={{0,30},{2,0},{4,2},{6,4},{8,6},{10,8},{12,10},{14,12},{16,14},{18,... | collective-permute-start | bytes 786440 | tf_op jit(solution)/shard_map/ppermute | solution.py:13
  345.8 3.3 collective-permute-done.14
  349.8 1.4 fusion.20
  351.7 6.1 %collective-permute-start.15 = (bf16[512,256]{1,0:T(8,128)(2,1)S(1)}, bf16[512,256]{1,0:T(8,128)(2,1)S(1)}, u32[]{:S(2)}, u32[]{:S(2)}) collective-permute-start(bf16[512,256]{1,0:T(8,128)(2,1)S(1)} %copy-done.20), channel_id=1, source_target_pairs={{0,30},{2,0},{4,2},{6,4},{8,6},{10,8},{12,10},{14,12},{16,14},{18,... | collective-permute-start | bytes 786440 | tf_op jit(solution)/shard_map/ppermute | solution.py:13
  358.5 3.3 collective-permute-done.15
  362.4 1.4 fusion.18
  365.0 4.8 %all-reduce.10 = (bf16[512,256]{1,0:T(8,128)(2,1)S(1)}, f32[256]{0:T(256)S(1)}) all-reduce(f32[512,256]{1,0:T(8,128)S(1)} %bitcast.296, f32[256]{0:T(256)S(1)} %copy-done.22), channel_id=1, replica_groups=mesh['row'=16,'rep'=2] {'rep'}, use_global_device_ids=true, to_apply=%region_1.3 | all-reduce | flops 131328 | bytes 788480 | tf_op jit(solution)/shard_map/psum | solution.py:52
  370.5 42.6 %psum.47 = f32[256]{0:T(256)S(1)} all-reduce(f32[256]{0:T(256)S(1)} %get-tuple-element.6), channel_id=1, replica_groups=mesh['row'=16,'rep'=2] {'row'}, use_global_device_ids=true, to_apply=%region_6.8 | all-reduce | flops 256 | bytes 2048 | tf_op jit(solution)/shard_map/psum | solution.py:96
  (190 shorter events, 65.9 us)
Async XLA Ops:
  7.2 141.9 %copy-start = (bf16[256,256]{1,0:T(8,128)(2,1)S(1)}, bf16[256,256]{1,0:T(8,128)(2,1)}, u32[]{:S(2)}) copy-start(bf16[256,256]{1,0:T(8,128)(2,1)} %param.13) | copy-start | bytes 393220
  7.2 165.6 %all-reduce.6.cloned.1.call-start = ((), (), s32[]{:S(2)}) async-start(), calls=%async_computation | async-start | bytes 524288 | tf_op jit(solution)/shard_map/psum | solution.py:97
  7.2 47.9 %collective-permute-start = (bf16[512,256]{1,0:T(8,128)(2,1)}, bf16[512,256]{1,0:T(8,128)(2,1)S(1)}, u32[]{:S(2)}, u32[]{:S(2)}) collective-permute-start(bf16[512,256]{1,0:T(8,128)(2,1)} %param.12), channel_id=1, source_target_pairs={{0,16},{2,18},{4,20},{6,22},{8,24},{10,26},{12,28},{14,30},{16,0},... | collective-permute-start | bytes 786440 | tf_op jit(solution)/shard_map/ppermute | solution.py:13
  56.1 8.4 %collective-permute-start.1 = (bf16[512,256]{1,0:T(8,128)(2,1)S(1)}, bf16[512,256]{1,0:T(8,128)(2,1)S(1)}, u32[]{:S(2)}, u32[]{:S(2)}) collective-permute-start(bf16[512,256]{1,0:T(8,128)(2,1)S(1)} %broadcast_select_fusion.1), channel_id=1, source_target_pairs={{0,30},{2,0},{4,2},{6,4},{8,6},{10,8},{12,10},{14,12},{16,14},{18,... | collective-permute-start | bytes 786440 | tf_op jit(solution)/shard_map/ppermute | solution.py:13
  67.0 10.3 %collective-permute-start.2 = (bf16[512,256]{1,0:T(8,128)(2,1)S(1)}, bf16[512,256]{1,0:T(8,128)(2,1)S(1)}, u32[]{:S(2)}, u32[]{:S(2)}) collective-permute-start(bf16[512,256]{1,0:T(8,128)(2,1)S(1)} %collective-permute-done.1), channel_id=1, source_target_pairs={{0,30},{2,0},{4,2},{6,4},{8,6},{10,8},{12,10},{14,12},{16,14},{18,... | collective-permute-start | bytes 786440 | tf_op jit(solution)/shard_map/ppermute | solution.py:13
  77.4 0.7 copy-start.1
  78.1 1.9 copy-start.2
  80.0 10.0 %collective-permute-start.3 = (bf16[512,256]{1,0:T(8,128)(2,1)S(1)}, bf16[512,256]{1,0:T(8,128)(2,1)S(1)}, u32[]{:S(2)}, u32[]{:S(2)}) collective-permute-start(bf16[512,256]{1,0:T(8,128)(2,1)S(1)} %copy-done.2), channel_id=1, source_target_pairs={{0,30},{2,0},{4,2},{6,4},{8,6},{10,8},{12,10},{14,12},{16,14},{18,... | collective-permute-start | bytes 786440 | tf_op jit(solution)/shard_map/ppermute | solution.py:13
  90.0 0.7 copy-start.3
  90.8 1.9 copy-start.4
  92.7 10.0 %collective-permute-start.4 = (bf16[512,256]{1,0:T(8,128)(2,1)S(1)}, bf16[512,256]{1,0:T(8,128)(2,1)S(1)}, u32[]{:S(2)}, u32[]{:S(2)}) collective-permute-start(bf16[512,256]{1,0:T(8,128)(2,1)S(1)} %copy-done.4), channel_id=1, source_target_pairs={{0,30},{2,0},{4,2},{6,4},{8,6},{10,8},{12,10},{14,12},{16,14},{18,... | collective-permute-start | bytes 786440 | tf_op jit(solution)/shard_map/ppermute | solution.py:13
  102.7 0.7 copy-start.5
  103.4 1.9 copy-start.6
  105.4 10.0 %collective-permute-start.5 = (bf16[512,256]{1,0:T(8,128)(2,1)S(1)}, bf16[512,256]{1,0:T(8,128)(2,1)S(1)}, u32[]{:S(2)}, u32[]{:S(2)}) collective-permute-start(bf16[512,256]{1,0:T(8,128)(2,1)S(1)} %copy-done.6), channel_id=1, source_target_pairs={{0,30},{2,0},{4,2},{6,4},{8,6},{10,8},{12,10},{14,12},{16,14},{18,... | collective-permute-start | bytes 786440 | tf_op jit(solution)/shard_map/ppermute | solution.py:13
  115.4 0.7 copy-start.7
  116.1 1.9 copy-start.8
  118.0 10.0 %collective-permute-start.6 = (bf16[512,256]{1,0:T(8,128)(2,1)S(1)}, bf16[512,256]{1,0:T(8,128)(2,1)S(1)}, u32[]{:S(2)}, u32[]{:S(2)}) collective-permute-start(bf16[512,256]{1,0:T(8,128)(2,1)S(1)} %copy-done.8), channel_id=1, source_target_pairs={{0,30},{2,0},{4,2},{6,4},{8,6},{10,8},{12,10},{14,12},{16,14},{18,... | collective-permute-start | bytes 786440 | tf_op jit(solution)/shard_map/ppermute | solution.py:13
  128.0 0.7 copy-start.9
  128.8 1.9 copy-start.10
  130.7 10.2 %collective-permute-start.7 = (bf16[512,256]{1,0:T(8,128)(2,1)S(1)}, bf16[512,256]{1,0:T(8,128)(2,1)S(1)}, u32[]{:S(2)}, u32[]{:S(2)}) collective-permute-start(bf16[512,256]{1,0:T(8,128)(2,1)S(1)} %copy-done.10), channel_id=1, source_target_pairs={{0,30},{2,0},{4,2},{6,4},{8,6},{10,8},{12,10},{14,12},{16,14},{18,... | collective-permute-start | bytes 786440 | tf_op jit(solution)/shard_map/ppermute | solution.py:13
  141.6 1.9 copy-start.28
  141.6 1.9 copy-start.35
  143.5 5.6 %copy-start.21 = (bf16[512,256]{1,0:T(8,128)(2,1)S(1)}, bf16[512,256]{1,0:T(8,128)(2,1)}, u32[]{:S(2)}) copy-start(bf16[512,256]{1,0:T(8,128)(2,1)} %all_gather.3) | copy-start | bytes 786436
  143.5 5.6 %copy-start.37 = (f32[256]{0:T(256)S(1)}, f32[256]{0:T(256)}, u32[]{:S(2)}) copy-start(f32[256]{0:T(256)} %param.14) | copy-start | bytes 3076
  149.5 16.7 %copy-start.34 = (pred[8]{0:T(512)(128)(4,1)S(1)}, pred[8]{0:T(512)(128)(4,1)}, u32[]{:S(2)}) copy-start(pred[8]{0:T(512)(128)(4,1)} %get-tuple-element.21) | copy-start | bytes 28
  149.8 9.6 %collective-permute-start.8 = (bf16[512,256]{1,0:T(8,128)(2,1)S(1)}, bf16[512,256]{1,0:T(8,128)(2,1)S(1)}, u32[]{:S(2)}, u32[]{:S(2)}) collective-permute-start(bf16[512,256]{1,0:T(8,128)(2,1)S(1)} %convolution_convert_fusion), channel_id=1, source_target_pairs={{0,16},{2,18},{4,20},{6,22},{8,24},{10,26},{12,28},{14,30},{16,0},... | collective-permute-start | bytes 786440 | tf_op jit(solution)/shard_map/ppermute | solution.py:13
  152.0 134.8 %all-reduce.8.cloned.1.call-start = ((), (), s32[]{:S(2)}) async-start(), calls=%async_computation.1 | async-start | bytes 524288 | tf_op jit(solution)/shard_map/psum | solution.py:96
  159.5 129.0 %collective-permute-start.9 = (bf16[512,256]{1,0:T(8,128)(2,1)S(1)}, bf16[512,256]{1,0:T(8,128)(2,1)S(1)}, u32[]{:S(2)}, u32[]{:S(2)}) collective-permute-start(bf16[512,256]{1,0:T(8,128)(2,1)S(1)} %broadcast_select_fusion), channel_id=1, source_target_pairs={{0,30},{2,0},{4,2},{6,4},{8,6},{10,8},{12,10},{14,12},{16,14},{18,... | collective-permute-start | bytes 786440 | tf_op jit(solution)/shard_map/ppermute | solution.py:13
  166.2 6.6 %copy-start.23 = (s32[8]{0:T(128)S(1)}, s32[8]{0:T(128)}, u32[]{:S(2)}) copy-start(s32[8]{0:T(128)} %get-tuple-element.89) | copy-start | bytes 100
  166.2 6.6 %copy-start.29 = (pred[8]{0:T(512)(128)(4,1)S(1)}, pred[8]{0:T(512)(128)(4,1)}, u32[]{:S(2)}) copy-start(pred[8]{0:T(512)(128)(4,1)} %iota_compare_fusion.23) | copy-start | bytes 28
  168.1 121.1 %copy-start.32 = (pred[8]{0:T(512)(128)(4,1)S(1)}, pred[8]{0:T(512)(128)(4,1)}, u32[]{:S(2)}) copy-start(pred[8]{0:T(512)(128)(4,1)} %get-tuple-element.19) | copy-start | bytes 28
  291.0 7.2 %collective-permute-start.10 = (bf16[512,256]{1,0:T(8,128)(2,1)S(1)}, bf16[512,256]{1,0:T(8,128)(2,1)S(1)}, u32[]{:S(2)}, u32[]{:S(2)}) collective-permute-start(bf16[512,256]{1,0:T(8,128)(2,1)S(1)} %collective-permute-done.9), channel_id=1, source_target_pairs={{0,30},{2,0},{4,2},{6,4},{8,6},{10,8},{12,10},{14,12},{16,14},{18,... | collective-permute-start | bytes 786440 | tf_op jit(solution)/shard_map/ppermute | solution.py:13
  298.2 0.7 copy-start.11
  298.9 1.9 copy-start.12
  300.9 10.0 %collective-permute-start.11 = (bf16[512,256]{1,0:T(8,128)(2,1)S(1)}, bf16[512,256]{1,0:T(8,128)(2,1)S(1)}, u32[]{:S(2)}, u32[]{:S(2)}) collective-permute-start(bf16[512,256]{1,0:T(8,128)(2,1)S(1)} %copy-done.12), channel_id=1, source_target_pairs={{0,30},{2,0},{4,2},{6,4},{8,6},{10,8},{12,10},{14,12},{16,14},{18,... | collective-permute-start | bytes 786440 | tf_op jit(solution)/shard_map/ppermute | solution.py:13
  310.9 0.7 copy-start.13
  311.6 1.9 copy-start.14
  313.5 10.0 %collective-permute-start.12 = (bf16[512,256]{1,0:T(8,128)(2,1)S(1)}, bf16[512,256]{1,0:T(8,128)(2,1)S(1)}, u32[]{:S(2)}, u32[]{:S(2)}) collective-permute-start(bf16[512,256]{1,0:T(8,128)(2,1)S(1)} %copy-done.14), channel_id=1, source_target_pairs={{0,30},{2,0},{4,2},{6,4},{8,6},{10,8},{12,10},{14,12},{16,14},{18,... | collective-permute-start | bytes 786440 | tf_op jit(solution)/shard_map/ppermute | solution.py:13
  323.6 0.7 copy-start.15
  324.3 8.3 %copy-start.25 = (s32[8]{0:T(128)S(1)}, s32[8]{0:T(128)}, u32[]{:S(2)}) copy-start(s32[8]{0:T(128)} %get-tuple-element.85) | copy-start | bytes 100
  324.3 1.9 copy-start.16
  326.2 10.2 %collective-permute-start.13 = (bf16[512,256]{1,0:T(8,128)(2,1)S(1)}, bf16[512,256]{1,0:T(8,128)(2,1)S(1)}, u32[]{:S(2)}, u32[]{:S(2)}) collective-permute-start(bf16[512,256]{1,0:T(8,128)(2,1)S(1)} %copy-done.16), channel_id=1, source_target_pairs={{0,30},{2,0},{4,2},{6,4},{8,6},{10,8},{12,10},{14,12},{16,14},{18,... | collective-permute-start | bytes 786440 | tf_op jit(solution)/shard_map/ppermute | solution.py:13
  336.4 0.7 copy-start.17
  337.1 8.1 %copy-start.24 = (s32[8]{0:T(128)S(1)}, s32[8]{0:T(128)}, u32[]{:S(2)}) copy-start(s32[8]{0:T(128)} %get-tuple-element.84) | copy-start | bytes 100
  337.1 8.1 %copy-start.33 = (pred[8]{0:T(512)(128)(4,1)S(1)}, pred[8]{0:T(512)(128)(4,1)}, u32[]{:S(2)}) copy-start(pred[8]{0:T(512)(128)(4,1)} %iota_compare_fusion.18) | copy-start | bytes 28
  337.2 1.9 copy-start.18
  339.1 10.0 %collective-permute-start.14 = (bf16[512,256]{1,0:T(8,128)(2,1)S(1)}, bf16[512,256]{1,0:T(8,128)(2,1)S(1)}, u32[]{:S(2)}, u32[]{:S(2)}) collective-permute-start(bf16[512,256]{1,0:T(8,128)(2,1)S(1)} %copy-done.18), channel_id=1, source_target_pairs={{0,30},{2,0},{4,2},{6,4},{8,6},{10,8},{12,10},{14,12},{16,14},{18,... | collective-permute-start | bytes 786440 | tf_op jit(solution)/shard_map/ppermute | solution.py:13
  349.1 0.7 copy-start.19
  349.8 8.1 %copy-start.27 = (s32[8]{0:T(128)S(1)}, s32[8]{0:T(128)}, u32[]{:S(2)}) copy-start(s32[8]{0:T(128)} %get-tuple-element.83) | copy-start | bytes 100
  349.8 8.1 %copy-start.31 = (pred[8]{0:T(512)(128)(4,1)S(1)}, pred[8]{0:T(512)(128)(4,1)}, u32[]{:S(2)}) copy-start(pred[8]{0:T(512)(128)(4,1)} %iota_compare_fusion.17) | copy-start | bytes 28
  349.8 1.9 copy-start.20
  351.7 10.6 %copy-start.30 = (pred[8]{0:T(512)(128)(4,1)S(1)}, pred[8]{0:T(512)(128)(4,1)}, u32[]{:S(2)}) copy-start(pred[8]{0:T(512)(128)(4,1)} %get-tuple-element.7) | copy-start | bytes 28
  351.7 10.0 %collective-permute-start.15 = (bf16[512,256]{1,0:T(8,128)(2,1)S(1)}, bf16[512,256]{1,0:T(8,128)(2,1)S(1)}, u32[]{:S(2)}, u32[]{:S(2)}) collective-permute-start(bf16[512,256]{1,0:T(8,128)(2,1)S(1)} %copy-done.20), channel_id=1, source_target_pairs={{0,30},{2,0},{4,2},{6,4},{8,6},{10,8},{12,10},{14,12},{16,14},{18,... | collective-permute-start | bytes 786440 | tf_op jit(solution)/shard_map/ppermute | solution.py:13
  362.3 1.9 copy-start.26
  362.4 1.9 copy-start.36
  364.2 0.8 copy-start.22
Sparse Core Ops, SparseCore 0:
  152.1 20.6 all-reduce.5
  178.8 107.8 all-reduce.7
